TPU v7x, 128 devices: a whole 4x4x4 slice. The times are simulated.
128 devices in a mesh: row: 8 (over z, core), col: 16 (over x, y).
Axes of the slice: x: 4, y: 4, z: 4, core: 2. Of those that a mesh axis runs over, the one named last changes fastest.
Arguments:
- tensor_blocks: bfloat16 [128, 16, 4, 128, 128], P(None, 'row', None, 'col'), may hold values from -0.25 to 0.25
- density: bfloat16 [2048, 2048], P(('row', 'col')), may hold values from -6 to 6
- coef: bfloat16 [128, 16, 4, 128, 128], P('col'), may hold values from -0.03125 to 0.03125
- lam_list: int32 [16, 4], P('row'), may hold values from 0 to 15, all different within a row
- sig_list: int32 [16, 4], replicated, may hold values from 0 to 15, all different within a row
Outputs:
- exchange_matrix: float32 [2048, 2048], P('col', 'row')
Inputs may be any that keep to these rules, and one draw needn't show every extreme that they name: `lam_list`: each row names 4 different tiles, and every tile is named by some row. `sig_list`: each row names 4 different tiles, and every tile is named by some row.
All inputs are finite; a program needn't handle non-finite values.
Results may differ from a plain program's by a relative error of at most 0.0029.
Values may be sent and summed in bfloat16 or wider, within the bound.
A program may use at most 128 MiB of HBM per device.

v0:
```python
import jax
import jax.numpy as jnp
from jax import lax
from jax.sharding import PartitionSpec as P


def per_device(tensor_blocks, density, coef, lam_list, sig_list):
    gathered = lax.all_gather(density, ("row", "col"), axis=0, tiled=True)
    basis_count = gathered.shape[0]
    tile_width = tensor_blocks.shape[-1]
    tile_count = basis_count // tile_width
    density_tiles = gathered.reshape(tile_count, tile_width, basis_count)
    tile_rows = density_tiles[lam_list]
    local_products = jnp.einsum(
        "atkij,tkjn->atin", tensor_blocks, tile_rows, preferred_element_type=jnp.float32
    ).astype(jnp.bfloat16)
    products = lax.all_to_all(local_products, "col", split_axis=0, concat_axis=2, tiled=True)
    aux_count = products.shape[0]
    mu_rows = products.shape[1] * products.shape[2]
    by_tile = products.reshape(aux_count, mu_rows, tile_count, tile_width)
    picked = jnp.take(by_tile, sig_list, axis=2)
    partial_sum = jnp.einsum("amukj,aukij->uim", picked, coef, preferred_element_type=jnp.float32)
    return lax.psum_scatter(
        partial_sum.reshape(basis_count // lax.axis_size("col") * lax.axis_size("col"), mu_rows),
        "col",
        scatter_dimension=0,
        tiled=True,
    )


def solution(mesh):
    in_specs = (
        P(None, "row", None, "col", None),
        P(("row", "col"), None),
        P("col", None, None, None, None),
        P("row", None),
        P(),
    )
    out_specs = P("col", "row")
    return jax.shard_map(
        per_device, mesh=mesh, in_specs=in_specs, out_specs=out_specs, check_vma=False
    )
```

profile of v0, /device:TPU:1, one launch (start us, length us, event | category | flops | bytes accessed | tf_op | source)
XLA Modules:
  0.0 415.6 jit_solution(13787731798977825657)
XLA Ops:
  6.5 0.0 copy-start
  6.5 0.0 all-gather.2.cloned.1.call-start
  6.5 0.7 all-gather.2.cloned.1.call-update
  7.3 0.7 compare_select_fusion.1
  7.9 0.1 reshape.20
  8.0 76.3 %all-gather.2.cloned.1.call-done = bf16[2048,2048]{1,0:T(8,128)(2,1)} async-done(((bf16[16,2048]{1,0:T(8,128)(2,1)}), bf16[2048,2048]{1,0:T(8,128)(2,1)}) %all-gather.2.cloned.1.call-update) | async-done | bytes 8388624 | tf_op jit(solution)/shard_map/all_gather | solution.py:8
  84.3 6.2 %gather_fusion = bf16[8,128,2048]{2,1,0:T(8,128)(2,1)} fusion(bf16[16,128,2048]{2,1,0:T(8,128)(2,1)} %bitcast.39, s32[1024]{0:T(1024)S(1)} %pad_clamp_fusion.1), kind=kCustom, calls=%fused_computation | custom fusion | bytes 8388640 | tf_op jit(solution)/shard_map/gather | solution.py:13
  90.5 0.0 copy-done
  90.5 11.6 %fusion.3 = bf16[128,2,8,2048]{0,3,2,1:T(8,128)(2,1)} fusion(bf16[2,4,128,2048,1]{3,2,1,4,0:T(8,128)(2,1)} %bitcast.38, bf16[128,2,4,8,128]{4,3,2,1,0:T(8,128)(2,1)S(1)} %copy-done), kind=kOutput, calls=%fused_computation.7 | convolution fusion | flops 4299161600 | bytes 14680064 | tf_op jit(solution)/shard_map/atkij,tkjn->atin/dot_general | solution.py:14
  102.0 12.5 %copy.23 = bf16[128,2,8,2048]{3,2,1,0:T(8,128)(2,1)} copy(bf16[128,2,8,2048]{0,3,2,1:T(8,128)(2,1)} %fusion.3) | data formatting | bytes 16777216 | tf_op jit(solution)/shard_map/convert_element_type | solution.py:16
  114.5 0.0 copy-start.2
  114.5 4.9 %all-to-all-start = ((bf16[128,2,8,2048]{3,2,1,0:T(8,128)(2,1)}), bf16[128,2,8,2048]{3,2,1,0:T(8,128)(2,1)}, u32[]{:S(2)}, u32[]{:S(2)}) async-start(bf16[128,2,8,2048]{3,2,1,0:T(8,128)(2,1)} %copy.23), calls=%async_computation | async-start | bytes 16777216 | tf_op jit(solution)/shard_map/all_to_all | solution.py:17
  119.4 0.2 reduce-scatter.2.cloned.1.call-start
  119.7 0.0 copy-done.2
  119.7 0.1 copy.25
  119.8 0.1 reshape.28
  119.9 0.1 copy.20
  120.0 146.9 %all-to-all-done = bf16[128,2,8,2048]{3,2,1,0:T(8,128)(2,1)} async-done(((bf16[128,2,8,2048]{3,2,1,0:T(8,128)(2,1)}), bf16[128,2,8,2048]{3,2,1,0:T(8,128)(2,1)}, u32[]{:S(2)}, u32[]{:S(2)}) %all-to-all-start) | async-done | bytes 8388640 | tf_op jit(solution)/shard_map/all_to_all | solution.py:17
  266.8 8.3 %copy.24 = bf16[8,2,16,8,2048]{4,3,2,1,0:T(8,128)(2,1)} copy(bf16[8,2,16,8,2048]{4,3,1,0,2:T(8,128)(2,1)} %bitcast.8) | data formatting | bytes 16777216 | tf_op jit(solution)/shard_map/all_to_all | solution.py:17
  275.1 9.8 %copy.32 = bf16[256,8,16,128]{3,2,1,0:T(8,128)(2,1)} copy(bf16[256,8,16,128]{3,1,2,0:T(8,128)(2,1)} %bitcast.36) | data formatting | bytes 16777216
  284.9 8.9 %copy.26 = bf16[8,256,16,128]{3,1,2,0:T(8,128)(2,1)} copy(bf16[8,256,16,128]{3,2,1,0:T(8,128)(2,1)} %bitcast.37) | data formatting | bytes 16777216 | tf_op jit(solution)/shard_map/reshape | solution.py:20
  293.8 15.7 %gather_fusion.1 = bf16[64,8,256,128]{3,2,1,0:T(8,128)(2,1)} fusion(bf16[8,256,16,128]{3,1,2,0:T(8,128)(2,1)} %copy.26, s32[1024]{0:T(1024)S(1)} %pad_clamp_fusion), kind=kCustom, calls=%fused_computation.1 | custom fusion | bytes 67109120 | tf_op jit(solution)/shard_map/jit(_take)/gather | solution.py:21
  309.6 0.0 copy-start.1
  309.6 20.6 %fusion = f32[16,256,128,1,1]{1,2,3,0,4:T(8,128)} fusion(bf16[8,16,4,128,128]{4,3,2,1,0:T(8,128)(2,1)} %param.7, bf16[16,4,8,256,128]{4,3,2,1,0:T(8,128)(2,1)} %bitcast.35, pred[16,4]{1,0:T(8,128)(4,1)S(1)} %copy.20), kind=kOutput, calls=%fused_computation.2 | convolution fusion | flops 4311744512 | bytes 52428864 | tf_op jit(solution)/shard_map/amukj,aukij->uim/dot_general | solution.py:22
  330.1 0.0 reduce-scatter.2.cloned.1.call-update
  330.2 78.6 %reduce-scatter.2.cloned.1.call-done = f32[128,256]{1,0:T(8,128)} async-done(((f32[2048,256]{1,0:T(8,128)}), f32[128,256]{1,0:T(8,128)}) %reduce-scatter.2.cloned.1.call-update) | async-done | bytes 131088 | tf_op jit(solution)/shard_map/reduce_scatter | solution.py:23
  408.8 0.0 copy-done.1
  (4 shorter events, 0.0 us)
Async XLA Ops:
  6.5 83.9 %copy-start = (bf16[128,2,4,8,128]{4,3,2,1,0:T(8,128)(2,1)S(1)}, bf16[128,2,4,8,128]{4,3,2,1,0:T(8,128)(2,1)}, u32[]{:S(2)}) copy-start(bf16[128,2,4,8,128]{4,3,2,1,0:T(8,128)(2,1)} %param.5) | copy-start | bytes 6291460
  6.5 77.8 %all-gather.2.cloned.1.call-start = ((), (), s32[]{:S(2)}) async-start(), calls=%async_computation.2 | async-start | bytes 8454144 | tf_op jit(solution)/shard_map/all_gather | solution.py:8
  114.5 5.1 %copy-start.2 = (s32[16,4]{0,1:T(4,128)S(1)}, s32[16,4]{0,1:T(4,128)}, u32[]{:S(2)}) copy-start(s32[16,4]{0,1:T(4,128)} %param.9) | copy-start | bytes 772
  114.5 152.3 %all-to-all-start = ((bf16[128,2,8,2048]{3,2,1,0:T(8,128)(2,1)}), bf16[128,2,8,2048]{3,2,1,0:T(8,128)(2,1)}, u32[]{:S(2)}, u32[]{:S(2)}) async-start(bf16[128,2,8,2048]{3,2,1,0:T(8,128)(2,1)} %copy.23), calls=%async_computation | async-start | bytes 16777216 | tf_op jit(solution)/shard_map/all_to_all | solution.py:17
  119.4 289.4 %reduce-scatter.2.cloned.1.call-start = ((), (), s32[]{:S(2)}) async-start(), calls=%async_computation.3 | async-start | bytes 2228224 | tf_op jit(solution)/shard_map/reduce_scatter | solution.py:23
  309.6 99.2 %copy-start.1 = (bf16[128,2,4,8,128]{4,3,2,1,0:T(8,128)(2,1)S(1)}, bf16[128,2,4,8,128]{4,3,2,1,0:T(8,128)(2,1)}, u32[]{:S(2)}) copy-start(bf16[128,2,4,8,128]{4,3,2,1,0:T(8,128)(2,1)} %param.5) | copy-start | bytes 6291460
Sparse Core Ops, SparseCore 0:
  10.5 73.7 all-gather.1
  330.3 78.4 reduce-scatter.1
where the time goes:
time: 417 us; the launch traced here: 416 us
  waiting for transfers between devices  303 us (73%)
  local copies, waits for them, and re-layouts  61.7 us (15%)
  matrix products  32.1 us (8%)
  between operations  13.4 us (3%)
  starting transfers between devices  5.11 us (1%)
    all_to_all x1, waiting for transfers between devices, per_device(): lax.all_to_all(local_products, 'col', split_axis=0, concat_axis=2, tiled=...  147 us
    reduce_scatter x1, waiting for transfers between devices, per_device(): lax.psum_scatter(partial_sum.reshape(basis_count // lax.axis_size('col')...  78.6 us
    all_gather x1, waiting for transfers between devices, per_device(): gathered = lax.all_gather(density, ('row', 'col'), axis=0, tiled=True)  76.3 us
    dot_general x1, matrix products, per_device(): jnp.einsum('amukj,aukij->uim', picked, coef, preferred_element_type=jnp.f...  20.6 us
    gather x1, local copies, waits for them, and re-layouts, per_device(): picked = jnp.take(by_tile, sig_list, axis=2)  15.7 us
    convert_element_type x1, local copies, waits for them, and re-layouts, per_device(): local_products = jnp.einsum('atkij,tkjn->atin', tensor_blocks, tile_rows,...  12.5 us
    dot_general x1, matrix products, per_device(): jnp.einsum('atkij,tkjn->atin', tensor_blocks, tile_rows, preferred_elemen...  11.6 us
    unnamed x7, local copies, waits for them, and re-layouts  9.78 us
  transfers between devices with their start and end apart: 3, of which 3 were waited for; matrix products, arithmetic and copies ran while one was open for 0% of the time, Pallas kernels for 0%

commit v1 on v0

v1 whole, which is shorter than its diff:
```python
import jax
import jax.numpy as jnp
from jax import lax
from jax.sharding import PartitionSpec as P


def per_device(tensor_blocks, density, coef, lam_list, sig_list):
    gathered = lax.all_gather(density, ("row", "col"), axis=0, tiled=True)
    basis_count = gathered.shape[0]
    tile_width = tensor_blocks.shape[-1]
    tile_count = basis_count // tile_width
    tile_rows = gathered.reshape(tile_count, tile_width, basis_count)[lam_list]
    blocks = lax.all_to_all(tensor_blocks, "col", split_axis=0, concat_axis=3, tiled=True)
    products = jnp.einsum("atkij,tkjn->atin", blocks, tile_rows, preferred_element_type=jnp.float32).astype(jnp.bfloat16)
    aux_count = products.shape[0]
    mu_rows = products.shape[1] * products.shape[2]
    by_tile = products.reshape(aux_count, mu_rows, tile_count, tile_width)
    picked = jnp.take(by_tile, sig_list, axis=2)
    partial_sum = jnp.einsum("amukj,aukij->uim", picked, coef, preferred_element_type=jnp.float32)
    return lax.psum_scatter(partial_sum.reshape(basis_count, mu_rows), "col", scatter_dimension=0, tiled=True)


def solution(mesh):
    in_specs = (
        P(None, "row", None, "col", None),
        P(("row", "col"), None),
        P("col", None, None, None, None),
        P("row", None),
        P(),
    )
    return jax.shard_map(per_device, mesh=mesh, in_specs=in_specs, out_specs=P("col", "row"), check_vma=False)
```

time: 417 us -> 255 us (0.61)
  waiting for transfers between devices: 303 us -> 147 us
  local copies, waits for them, and re-layouts: 61.7 us -> 52.4 us
    all_to_all x1, waiting for transfers between devices: 147 us -> 0.01 us  [per_device(): lax.all_to_all(tensor_blocks, 'col', split_axis=0, concat_axis=3, tiled=T...]
    reduce_scatter x1, waiting for transfers between devices: 78.6 us -> 69.8 us  [per_device(): lax.psum_scatter(partial_sum.reshape(basis_count, mu_rows), 'col', scatte...]
    all_to_all x1 -> x0, local copies, waits for them, and re-layouts: 8.28 us -> none  [per_device(): lax.all_to_all(local_products, 'col', split_axis=0, concat_axis=2, tiled=...]
    unnamed x7 -> x1, local copies, waits for them, and re-layouts: 9.78 us -> 9.77 us
  transfers between devices with their start and end apart: 3 -> 3, of which waited for: 3 -> 2; matrix products, arithmetic and copies ran while one was open for 0% -> 3% of each run, Pallas kernels for 0% -> 0%
where the time goes in v1:
time: 255 us; the launch traced here: 253 us
  waiting for transfers between devices  147 us (58%)
  local copies, waits for them, and re-layouts  52.4 us (21%)
  matrix products  30.7 us (12%)
  between operations  13.4 us (5%)
  starting transfers between devices  7.64 us (3%)
    all_gather x1, waiting for transfers between devices, per_device(): gathered = lax.all_gather(density, ('row', 'col'), axis=0, tiled=True)  76.7 us
    reduce_scatter x1, waiting for transfers between devices, per_device(): lax.psum_scatter(partial_sum.reshape(basis_count, mu_rows), 'col', scatte...  69.8 us
    dot_general x1, matrix products, per_device(): jnp.einsum('amukj,aukij->uim', picked, coef, preferred_element_type=jnp.f...  20.3 us
    gather x1, local copies, waits for them, and re-layouts, per_device(): picked = jnp.take(by_tile, sig_list, axis=2)  15.8 us
    convert_element_type x1, local copies, waits for them, and re-layouts, per_device(): jnp.einsum('atkij,tkjn->atin', blocks, tile_rows, preferred_element_type=...  11.5 us
    dot_general x1, matrix products, per_device(): jnp.einsum('atkij,tkjn->atin', blocks, tile_rows, preferred_element_type=...  10.3 us
    unnamed x1, local copies, waits for them, and re-layouts  9.77 us
    reshape x1, local copies, waits for them, and re-layouts, per_device(): by_tile = products.reshape(aux_count, mu_rows, tile_count, tile_width)  8.93 us
  transfers between devices with their start and end apart: 3, of which 2 were waited for; matrix products, arithmetic and copies ran while one was open for 3% of the time, Pallas kernels for 0%

profile of v1, /device:TPU:1, one launch (start us, length us, event | category | flops | bytes accessed | tf_op | source)
XLA Modules:
  0.0 253.5 jit_solution(17438284669154244088)
XLA Ops:
  6.5 0.0 all-gather.2.cloned.1.call-start
  6.5 0.7 all-gather.2.cloned.1.call-update
  7.3 7.6 %all-to-all-start = ((bf16[128,2,4,8,128]{4,3,2,1,0:T(8,128)(2,1)}), bf16[128,2,4,8,128]{4,3,2,1,0:T(8,128)(2,1)S(1)}, u32[]{:S(2)}, u32[]{:S(2)}) async-start(bf16[128,2,4,8,128]{4,3,2,1,0:T(8,128)(2,1)} %param.5), calls=%async_computation | async-start | bytes 4194304 | tf_op jit(solution)/shard_map/all_to_all | solution.py:13
  14.9 0.0 reduce-scatter.2.cloned.1.call-start
  14.9 0.7 compare_select_fusion.1
  15.6 0.1 reshape.19
  15.7 0.7 compare_select_fusion
  16.4 0.1 copy.15
  16.4 0.1 reshape.27
  16.5 0.7 compare_and_fusion
  17.2 0.1 copy.11
  17.3 76.7 %all-gather.2.cloned.1.call-done = bf16[2048,2048]{1,0:T(8,128)(2,1)} async-done(((bf16[16,2048]{1,0:T(8,128)(2,1)}), bf16[2048,2048]{1,0:T(8,128)(2,1)}) %all-gather.2.cloned.1.call-update) | async-done | bytes 8388624 | tf_op jit(solution)/shard_map/all_gather | solution.py:8
  94.0 6.1 %gather_fusion = bf16[8,128,2048]{2,1,0:T(8,128)(2,1)} fusion(bf16[16,128,2048]{2,1,0:T(8,128)(2,1)} %bitcast.42, s32[1024]{0:T(1024)S(1)} %pad_clamp_fusion.1), kind=kCustom, calls=%fused_computation | custom fusion | bytes 8388640 | tf_op jit(solution)/shard_map/gather | solution.py:12
  100.2 0.0 all-to-all-done
  100.2 10.3 %fusion.3 = bf16[8,2,128,2048]{2,3,0,1:T(8,128)(2,1)} fusion(bf16[2,4,128,2048,1]{3,2,1,4,0:T(8,128)(2,1)} %bitcast.41, bf16[16,8,2,4,8,128]{5,4,3,2,1,0:T(8,128)(2,1)S(1)} %bitcast.43), kind=kOutput, calls=%fused_computation.7 | convolution fusion | flops 4299161600 | bytes 14680064 | tf_op jit(solution)/shard_map/atkij,tkjn->atin/dot_general | solution.py:14
  110.5 11.5 %copy.14 = bf16[8,2,128,2048]{3,2,1,0:T(8,128)(2,1)} copy(bf16[8,2,128,2048]{2,3,0,1:T(8,128)(2,1)} %fusion.3) | data formatting | bytes 16777216 | tf_op jit(solution)/shard_map/convert_element_type | solution.py:14
  122.0 9.8 %copy.26 = bf16[256,8,16,128]{3,2,1,0:T(8,128)(2,1)} copy(bf16[256,8,16,128]{3,1,2,0:T(8,128)(2,1)} %bitcast.39) | data formatting | bytes 16777216
  131.8 8.9 %copy.16 = bf16[8,256,16,128]{3,1,2,0:T(8,128)(2,1)} copy(bf16[8,256,16,128]{3,2,1,0:T(8,128)(2,1)} %bitcast.40) | data formatting | bytes 16777216 | tf_op jit(solution)/shard_map/reshape | solution.py:17
  140.7 15.8 %gather_fusion.1 = bf16[64,8,256,128]{3,2,1,0:T(8,128)(2,1)} fusion(bf16[8,256,16,128]{3,1,2,0:T(8,128)(2,1)} %copy.16, s32[1024]{0:T(1024)S(1)} %pad_clamp_fusion), kind=kCustom, calls=%fused_computation.1 | custom fusion | bytes 67109120 | tf_op jit(solution)/shard_map/jit(_take)/gather | solution.py:18
  156.5 20.3 %fusion = f32[16,256,128,1,1]{1,2,3,0,4:T(8,128)} fusion(bf16[8,16,4,128,128]{4,3,2,1,0:T(8,128)(2,1)} %param.7, bf16[16,4,8,256,128]{4,3,2,1,0:T(8,128)(2,1)} %bitcast.38, pred[16,4]{1,0:T(8,128)(4,1)S(1)} %copy.11), kind=kOutput, calls=%fused_computation.2 | convolution fusion | flops 4311744512 | bytes 52428864 | tf_op jit(solution)/shard_map/amukj,aukij->uim/dot_general | solution.py:19
  176.8 0.0 reduce-scatter.2.cloned.1.call-update
  176.8 69.8 %reduce-scatter.2.cloned.1.call-done = f32[128,256]{1,0:T(8,128)} async-done(((f32[2048,256]{1,0:T(8,128)}), f32[128,256]{1,0:T(8,128)}) %reduce-scatter.2.cloned.1.call-update) | async-done | bytes 131088 | tf_op jit(solution)/shard_map/reduce_scatter | solution.py:20
  (2 shorter events, 0.0 us)
Async XLA Ops:
  6.5 87.5 %all-gather.2.cloned.1.call-start = ((), (), s32[]{:S(2)}) async-start(), calls=%async_computation.2 | async-start | bytes 8454144 | tf_op jit(solution)/shard_map/all_gather | solution.py:8
  7.3 92.9 %all-to-all-start = ((bf16[128,2,4,8,128]{4,3,2,1,0:T(8,128)(2,1)}), bf16[128,2,4,8,128]{4,3,2,1,0:T(8,128)(2,1)S(1)}, u32[]{:S(2)}, u32[]{:S(2)}) async-start(bf16[128,2,4,8,128]{4,3,2,1,0:T(8,128)(2,1)} %param.5), calls=%async_computation | async-start | bytes 4194304 | tf_op jit(solution)/shard_map/all_to_all | solution.py:13
  14.9 231.8 %reduce-scatter.2.cloned.1.call-start = ((), (), s32[]{:S(2)}) async-start(), calls=%async_computation.3 | async-start | bytes 2228224 | tf_op jit(solution)/shard_map/reduce_scatter | solution.py:20
Sparse Core Ops, SparseCore 0:
  10.5 83.5 all-gather.1
  177.0 69.6 reduce-scatter.1

commit v2 on v1

v2 whole, which is shorter than its diff:
```python
import functools

import jax
import jax.numpy as jnp
from jax import lax
from jax.experimental import pallas as pl
from jax.experimental.pallas import tpu as pltpu
from jax.sharding import PartitionSpec as P

MESH = pl.DeviceIdType.MESH
F32, BF16 = jnp.float32, jnp.bfloat16
OPT = dict(D=True, T=True, S1=True, S2=True, K=True, groups=2, parts=((0, 512), (512, 512), (1024, 1024)), t_late=False)
ORDERS = (("y", "z", "x"), ("z", "x", "y"), ("x", "y", "z"))


def kernel(opt, lam_ref, sig_ref, t_hbm, d_hbm, c_hbm, out_ref, dbuf, cbuf, rbuf, tl, prod, kacc, kbf, krecv,
           d_send, d_recv, t_send, t_recv, k_send, k_recv, loc_sem, c_sem):
    groups = opt["groups"]
    pg = 8 // groups
    r, c = lax.axis_index("row"), lax.axis_index("col")
    z, core, x, y = r // 2, r % 2, c // 4, c % 4
    here = {"x": x, "y": y, "z": z}

    def peer(axis, step):
        n = lax.rem(here[axis] + step + 4, 4)
        if axis == "z":
            return (n * 2 + core, c)
        return (r, n * 4 + y) if axis == "x" else (r, x * 4 + n)

    sibling = (r + 1 - 2 * core, c)

    for p in range(8):
        pltpu.make_async_copy(c_hbm.at[p], cbuf.at[p], c_sem.at[p]).start()
    own_d = pltpu.make_async_copy(d_hbm, dbuf.at[z, core, x, y], loc_sem.at[0])
    own_d.start()
    own_t = pltpu.make_async_copy(t_hbm.at[pl.ds(c * 8, 8)], rbuf.at[c], loc_sem.at[1])
    own_t.start()

    barrier = pltpu.get_barrier_semaphore()

    @pl.loop(1, 16)
    def _(i):
        pl.semaphore_signal(barrier, inc=1, device_id=(r, lax.rem(c + i, 16)), device_id_type=MESH)

    for dev in (peer("z", 1), peer("z", -1), sibling):
        pl.semaphore_signal(barrier, inc=1, device_id=dev, device_id_type=MESH)
    pl.semaphore_wait(barrier, 18)

    def t_copy(g, dst, src):
        return pltpu.make_async_remote_copy(
            src_ref=t_hbm.at[pl.ds(dst * 8 + g * pg, pg)], dst_ref=rbuf.at[src, pl.ds(g * pg, pg)],
            send_sem=t_send.at[g, dst], recv_sem=t_recv.at[g, src], device_id=(r, dst), device_id_type=MESH)

    def t_start():
        for g in range(groups):
            @pl.loop(1, 16)
            def _(i):
                t_copy(g, lax.rem(c + i, 16), c).start()

    own_d.wait()

    def region(part, done, at, core_at, sub=None):
        first, width = opt["parts"][part]
        if sub is not None:
            half = (width // 256) * 128
            first, width = (first, half) if sub == 0 else (first + half, width - half)
        pos = {a: (slice(None) if a in done else at.get(a, here[a])) for a in "xyz"}
        return dbuf.at[pos["z"], core_at, pos["x"], pos["y"], :, pl.ds(first, width)]

    def d_copy(ref, s, dev):
        return pltpu.make_async_remote_copy(src_ref=ref, dst_ref=ref, send_sem=d_send.at[s], recv_sem=d_recv.at[s],
                                            device_id=dev, device_id_type=MESH)

    started = []
    sib_wait = []

    def wait_recv(ref, s):
        pltpu.make_async_copy(ref, ref, d_recv.at[s]).wait()

    def to_sibling(part, done, at, sub, s):
        cp = d_copy(region(part, done, at, core, sub), s, sibling)
        cp.start()
        started.append(cp)
        sib_wait.append((region(part, done, at, 1 - core, sub), s))

    if opt["D"]:
        if not opt["t_late"] and opt["T"]:
            t_start()
        nparts = range(len(opt["parts"]))
        for phase in range(3):
            for p in nparts:
                done, axis = ORDERS[p][:phase], ORDERS[p][phase]
                base = p * 17 + phase * 4
                for j, step in enumerate((1, -1)):
                    cp = d_copy(region(p, done, {}, core), base + j, peer(axis, step))
                    cp.start()
                    started.append(cp)
            if phase == 2:
                for p in nparts:
                    to_sibling(p, ORDERS[p][:phase], {}, None, p * 17 + 12)
            for p in nparts:
                done, axis = ORDERS[p][:phase], ORDERS[p][phase]
                base = p * 17 + phase * 4
                for j, step in enumerate((1, -1)):
                    at = {axis: lax.rem(here[axis] - step + 4, 4)}
                    wait_recv(region(p, done, at, core), base + j)
                    cp = d_copy(region(p, done, at, core, j), base + 2 + j, peer(axis, step))
                    cp.start()
                    started.append(cp)
                    if phase == 2:
                        to_sibling(p, done, at, None, p * 17 + 13 + j)
            for p in nparts:
                done, axis = ORDERS[p][:phase], ORDERS[p][phase]
                base = p * 17 + phase * 4
                for j in range(2):
                    at = {axis: lax.rem(here[axis] + 2, 4)}
                    wait_recv(region(p, done, at, core, j), base + 2 + j)
                    if phase == 2:
                        to_sibling(p, done, at, j, p * 17 + 15 + j)
        if opt["t_late"] and opt["T"]:
            t_start()
        for ref, s in sib_wait:
            wait_recv(ref, s)
    elif opt["T"]:
        t_start()
    own_t.wait()

    for g in range(groups):
        if opt["T"]:
            @pl.loop(1, 16)
            def _(i):
                t_copy(g, c, lax.rem(c + i, 16)).wait_recv()
        if opt["S1"]:
            for t in range(2):
                for p in range(g * pg, (g + 1) * pg):
                    for kk in range(2):
                        both = rbuf[:, p, (t * 2 + kk) * 16:(t * 2 + kk + 1) * 16, :].astype(F32).reshape(16, 2, 8, 128)
                        for h in range(2):
                            tl[t, pl.ds((p - g * pg) * 128, 128), pl.ds((kk * 2 + h) * 128, 128)] = both[:, h].reshape(128, 128).astype(BF16)
            for t in range(2):
                lams = [lam_ref[t, k] for k in range(4)]

                @pl.loop(0, 2048 // opt.get("ncol", 256))
                def _(n):
                    nc = opt.get("ncol", 256)
                    cols = pl.ds(pl.multiple_of(n * nc, nc), nc)
                    rhs = jnp.concatenate(
                        [dbuf[lam // 4, (lam // 2) % 2, pl.ds((lam % 2) * 2, 2), :, :, cols].reshape(128, nc) for lam in lams], axis=0)
                    res = jnp.dot(tl[t], rhs, preferred_element_type=F32).astype(BF16)
                    for p in range(pg):
                        for h in range(nc // 128):
                            prod[g * pg + p, n * (nc // 128) + h, pl.ds(t * 128, 128), :] = res[p * 128:(p + 1) * 128, h * 128:(h + 1) * 128]
        for p in range(g * pg, (g + 1) * pg):
            pltpu.make_async_copy(c_hbm.at[p], cbuf.at[p], c_sem.at[p]).wait()

        @pl.loop(1, 17)
        def _(i):
            nu = lax.rem(c + i, 16)
            if opt["S2"]:
                sigs = [sig_ref[k, nu] for k in range(4)]
                lhs = jnp.concatenate([cbuf[p, nu, k] for p in range(g * pg, (g + 1) * pg) for k in range(4)], axis=1)
                rhs = jnp.concatenate([prod[p, s] for p in range(g * pg, (g + 1) * pg) for s in sigs], axis=1)
                acc = lax.dot_general(lhs, rhs, (((1,), (1,)), ((), ())), preferred_element_type=F32)
                if g > 0:
                    acc += kacc[nu]
                if g < groups - 1:
                    kacc[nu] = acc
            if g == groups - 1:
                if opt["S2"]:
                    kbf[nu] = acc.astype(BF16)
                if opt["K"]:
                    @pl.when(nu != c)
                    def _():
                        pltpu.make_async_remote_copy(
                            src_ref=kbf.at[nu], dst_ref=krecv.at[c], send_sem=k_send.at[nu], recv_sem=k_recv.at[c],
                            device_id=(r, nu), device_id_type=MESH).start()

                    @pl.when(nu == c)
                    def _():
                        out_ref[...] = acc if opt["S2"] else jnp.zeros_like(out_ref)

    if opt["K"]:
        @pl.loop(1, 16)
        def _(i):
            src = lax.rem(c + i, 16)
            pltpu.make_async_remote_copy(
                src_ref=kbf.at[src], dst_ref=krecv.at[src], send_sem=k_send.at[src], recv_sem=k_recv.at[src],
                device_id=(r, src), device_id_type=MESH).wait_recv()
            out_ref[...] += krecv[src].astype(F32)

        @pl.loop(1, 16)
        def _(i):
            dst = lax.rem(c + i, 16)
            pltpu.make_async_remote_copy(
                src_ref=kbf.at[dst], dst_ref=krecv.at[c], send_sem=k_send.at[dst], recv_sem=k_recv.at[c],
                device_id=(r, dst), device_id_type=MESH).wait_send()
    else:
        out_ref[...] = kacc[0]
    for cp in started:
        cp.wait_send()
    if opt["T"]:
        for g in range(groups):
            @pl.loop(1, 16)
            def _(i):
                t_copy(g, lax.rem(c + i, 16), c).wait_send()


def per_device(opt, tensor_blocks, density, coef, lam_list, sig_list):
    groups = opt["groups"]
    pg = 8 // groups
    return pl.pallas_call(
        functools.partial(kernel, opt),
        out_shape=jax.ShapeDtypeStruct((128, 256), F32),
        in_specs=[pl.BlockSpec(memory_space=pltpu.SMEM)] * 2 + [pl.BlockSpec(memory_space=pl.ANY)] * 3,
        out_specs=pl.BlockSpec(memory_space=pltpu.VMEM),
        scratch_shapes=[
            pltpu.VMEM((4, 2, 4, 4, 16, 2048), BF16),
            pltpu.VMEM((8, 16, 4, 128, 128), BF16),
            pltpu.VMEM((16, 8, 64, 128), BF16),
            pltpu.VMEM((2, pg * 128, 512), BF16),
            pltpu.VMEM((8, 16, 256, 128), BF16),
            pltpu.VMEM((16, 128, 256), F32),
            pltpu.VMEM((16, 128, 256), BF16),
            pltpu.VMEM((16, 128, 256), BF16),
            pltpu.SemaphoreType.DMA((51,)),
            pltpu.SemaphoreType.DMA((51,)),
            pltpu.SemaphoreType.DMA((groups, 16)),
            pltpu.SemaphoreType.DMA((groups, 16)),
            pltpu.SemaphoreType.DMA((16,)),
            pltpu.SemaphoreType.DMA((16,)),
            pltpu.SemaphoreType.DMA((2,)),
            pltpu.SemaphoreType.DMA((8,)),
        ],
        compiler_params=pltpu.CompilerParams(collective_id=0, has_side_effects=True, vmem_limit_bytes=60 * 2**20),
        cost_estimate=pl.CostEstimate(flops=2**33, bytes_accessed=20 * 2**20, transcendentals=0),
    )(lam_list, sig_list.T, tensor_blocks.reshape(128, 64, 128), density, coef)


def solution(mesh, **kw):
    in_specs = (
        P(None, "row", None, "col", None),
        P(("row", "col"), None),
        P("col", None, None, None, None),
        P("row", None),
        P(),
    )
    return jax.shard_map(functools.partial(per_device, {**OPT, **kw}), mesh=mesh, in_specs=in_specs, out_specs=P("col", "row"), check_vma=False)
```

time: 255 us -> 113 us (0.44)
  waiting for transfers between devices: 147 us -> 0 us
  Pallas kernels: 0 us -> 111 us
  local copies, waits for them, and re-layouts: 52.4 us -> 1.57 us
  matrix products: 30.7 us -> 0 us
  between operations: 13.4 us -> 0.01 us
  starting transfers between devices: 7.64 us -> 0 us
    pallas_call x0 -> x1, Pallas kernels: none -> 111 us  [per_device(): pl.pallas_call(functools.partial(kernel, opt), out_shape=jax.ShapeDtypeSt...]
    all_gather x1 -> x0, waiting for transfers between devices: 76.7 us -> none  [per_device(): gathered = lax.all_gather(density, ('row', 'col'), axis=0, tiled=True)]
    reduce_scatter x1 -> x0, waiting for transfers between devices: 69.8 us -> none  [per_device(): lax.psum_scatter(partial_sum.reshape(basis_count, mu_rows), 'col', scatte...]
    dot_general x2 -> x0, matrix products: 30.7 us -> none  [the longest x1 20.3 us: per_device(): jnp.einsum('amukj,aukij->uim', picked, coef, preferred_element_type=jnp.f...]
    gather x2 -> x0, local copies, waits for them, and re-layouts: 21.9 us -> none  [the longest x1 15.8 us: per_device(): picked = jnp.take(by_tile, sig_list, axis=2)]
    convert_element_type x1 -> x0, local copies, waits for them, and re-layouts: 11.5 us -> none  [per_device(): jnp.einsum('atkij,tkjn->atin', blocks, tile_rows, preferred_element_type=...]
    reshape x1 -> x0, local copies, waits for them, and re-layouts: 8.93 us -> none  [per_device(): by_tile = products.reshape(aux_count, mu_rows, tile_count, tile_width)]
    unnamed x1, local copies, waits for them, and re-layouts: 9.77 us -> 1.57 us
  transfers between devices with their start and end apart: 3 -> 0, of which waited for: 2 -> 0; matrix products, arithmetic and copies ran while one was open for 3% -> 0% of each run, Pallas kernels for 0% -> 0%
where the time goes in v2:
time: 113 us
  Pallas kernels  111 us (98%)
  local copies, waits for them, and re-layouts  1.57 us (1%)
    pallas_call x1, Pallas kernels, per_device(): pl.pallas_call(functools.partial(kernel, opt), out_shape=jax.ShapeDtypeSt...  111 us

profile of v2, /device:TPU:1, one launch (start us, length us, event | category | flops | bytes accessed | tf_op | source)
XLA Modules:
  0.0 112.9 jit_solution(17883192215948418880)
XLA Ops:
  0.0 111.3 %shard_map.55 = f32[128,256]{1,0:T(8,128)} custom-call(s32[2,4]{1,0:T(2,128)} %lam_ref.1, s32[4,16]{1,0:T(4,128)} %bitcast.3, bf16[128,64,128]{2,1,0:T(8,128)(2,1)} %bitcast.2, bf16[16,2048]{1,0:T(8,128)(2,1)} %d_hbm.1, bf16[8,16,4,128,128]{4,3,2,1,0:T(8,128)(2,1)} %c_hbm.1), custom_call_target="tpu_custom_call" | custom-call | flops 8589934592 | bytes 20971520 | tf_op jit(solution)/shard_map/pallas_call | solution.py:211
  111.3 1.6 %copy.7 = f32[128,256]{1,0:T(8,128)} copy(f32[128,256]{1,0:T(8,128)} %shard_map.55) | data formatting | bytes 262144

commit v3 on v1

v3 whole, which is shorter than its diff:
```python
import functools

import jax
import jax.numpy as jnp
from jax import lax
from jax.experimental import pallas as pl
from jax.experimental.pallas import tpu as pltpu
from jax.sharding import PartitionSpec as P

MESH = pl.DeviceIdType.MESH
F32, BF16 = jnp.float32, jnp.bfloat16
PARTS = (("xyz", 0, 768), ("yxz", 768, 768), ("zxy", 1536, 256), ("zyx", 1792, 256))
ORDER = tuple(((i + i // 4) % 4, i % 4) for i in range(1, 16))
SCHED = (("1", 0), ("1", 1), ("1", 2), ("1", 3), ("1b", 0), ("1b", 1), ("1b", 2), ("1b", 3), ("T", 0, 2), ("2", 0), ("2", 1), ("2", 2), ("2", 3),
         ("T", 2, 4), ("C",), ("3", 2), ("3", 3), ("T", 4, 8), ("3", 0), ("3", 1), ("4", 2), ("4", 3), ("4", 0), ("4", 1), ("S",))
OPT = dict(S1=True, S2=True, K=True, pg=4, parts=PARTS, sched=SCHED, order=ORDER, bar=False, mid=13)


def kernel(opt, lam_ref, sig_ref, t_hbm, d_hbm, c_hbm, out_ref, cbuf, rbuf, tl, prod, kbf, krecv,
           d_send, d_recv, t_send, t_recv, k_send, k_recv, loc_sem, c_sem, kmid, ksum, m_recv, *dparts):
    parts, pg = opt["parts"], opt["pg"]
    r, c = lax.axis_index("row"), lax.axis_index("col")
    z, core, x, y = r // 2, r % 2, c // 4, c % 4
    here = {"x": x, "y": y, "z": z}

    def peer(axis, step):
        n = lax.rem(here[axis] + step + 4, 4)
        if axis == "z":
            return (n * 2 + core, c)
        return (r, n * 4 + y) if axis == "x" else (r, x * 4 + n)

    sibling = (r + 1 - 2 * core, c)

    own_d = [pltpu.make_async_copy(d_hbm.at[:, pl.ds(first, width)],
                                   dparts[p].at[here[order[2]], core, here[order[1]], here[order[0]]], loc_sem.at[p])
             for p, (order, first, width) in enumerate(parts)]
    for cp in own_d:
        cp.start()
    for p in range(8):
        pltpu.make_async_copy(t_hbm.at[c * 8 + p], rbuf.at[c, p], t_recv.at[p]).start()

    barrier = pltpu.get_barrier_semaphore()

    def greet(dev):
        pl.semaphore_signal(barrier, inc=1, device_id=dev, device_id_type=MESH)

    for axis in "xyz":
        for step in (1, 2, 3):
            greet(peer(axis, step))
    greet(sibling)
    if opt["bar"]:
        for dx in (1, 2, 3):
            for dy in (1, 2, 3):
                greet((r, lax.rem(x + dx, 4) * 4 + lax.rem(y + dy, 4)))
    pl.semaphore_wait(barrier, 19 if opt["bar"] else 10)

    def t_start(first, last):
        @pl.loop(first, last)
        def _(p):
            for dx, dy in opt["order"]:
                dst = lax.rem(x + dx, 4) * 4 + lax.rem(y + dy, 4)
                pltpu.make_async_remote_copy(src_ref=t_hbm.at[dst * 8 + p], dst_ref=rbuf.at[c, p], send_sem=t_send.at[p], recv_sem=t_recv.at[p],
                                             device_id=(r, dst), device_id_type=MESH).start()

    started = []
    sib_wait = {p: [] for p in range(len(parts))}
    NS = 16

    def d_start(ref, s, dev):
        cp = pltpu.make_async_remote_copy(src_ref=ref, dst_ref=ref, send_sem=d_send.at[s], recv_sem=d_recv.at[s],
                                          device_id=dev, device_id_type=MESH)
        cp.start()
        started.append(cp)

    def d_wait(ref, s):
        pltpu.make_async_copy(ref, ref, d_recv.at[s]).wait()

    def shifted(axis, step):
        return lax.rem(here[axis] + step + 4, 4)

    def level1(p, a, core_at=core):
        o = parts[p][0]
        return dparts[p].at[here[o[2]], core_at, here[o[1]], a]

    def level2(p, a):
        o = parts[p][0]
        return dparts[p].at[here[o[2]], core, a]

    def level3(p, a, core_at, half=None):
        ref = dparts[p].at[a, core_at]
        return ref if half is None else ref.at[pl.ds(half * 2, 2)]

    def to_sibling(p, a, half, j):
        d_start(level3(p, a, core, half), p * NS + 4 + j, sibling)
        sib_wait[p].append((level3(p, a, 1 - core, half), p * NS + 4 + j))

    STEPS = (1, -1, 2)
    ps = range(len(parts))

    def stage1(p):
        o, first, width = parts[p]
        for j, step in enumerate(STEPS):
            s = p * NS + 10 + j
            cp = pltpu.make_async_remote_copy(src_ref=d_hbm.at[:, pl.ds(first, width)], dst_ref=level1(p, here[o[0]]), send_sem=d_send.at[s],
                                              recv_sem=d_recv.at[s], device_id=peer(o[0], step), device_id_type=MESH)
            cp.start()
            started.append(cp)

    def stage1b(p):
        o = parts[p][0]
        own_d[p].wait()
        for j, step in enumerate(STEPS):
            d_wait(level1(p, shifted(o[0], -step)), p * NS + 10 + j)
        for j, step in enumerate(STEPS):
            d_start(level2(p, here[o[1]]), p * NS + 13 + j, peer(o[1], step))

    def stage2(p):
        o = parts[p][0]
        for j, step in enumerate(STEPS):
            d_wait(level2(p, shifted(o[1], -step)), p * NS + 13 + j)
        for j, step in enumerate((1, -1)):
            d_start(level3(p, here[o[2]], core), p * NS + j, peer(o[2], step))
        to_sibling(p, here[o[2]], None, 0)

    def stage3(p):
        o = parts[p][0]
        for j, step in enumerate((1, -1)):
            at = shifted(o[2], -step)
            d_wait(level3(p, at, core), p * NS + j)
            d_start(level3(p, at, core, j), p * NS + 2 + j, peer(o[2], step))
            to_sibling(p, at, None, 1 + j)

    def stage4(p):
        o = parts[p][0]
        for j in range(2):
            at = shifted(o[2], 2)
            d_wait(level3(p, at, core, j), p * NS + 2 + j)
            to_sibling(p, at, j, 3 + j)

    def c_start():
        for p in range(8):
            pltpu.make_async_copy(c_hbm.at[p], cbuf.at[p], c_sem.at[p]).start()

    def t_gather(p):
        pltpu.make_async_copy(rbuf.at[:, p], rbuf.at[:, p], t_recv.at[p]).wait()
        if opt["S1"]:
            for t in range(2):
                for kk in range(2):
                    both = rbuf[:, p, (t * 2 + kk) * 16:(t * 2 + kk + 1) * 16, :].astype(F32).reshape(16, 2, 8, 128)
                    for h in range(2):
                        tl[t, pl.ds(pl.multiple_of(p * 128, 128), 128), pl.ds((kk * 2 + h) * 128, 128)] = both[:, h].reshape(128, 128).astype(BF16)

    def lam_rows(p, lam, cols):
        o = parts[p][0]
        pos = {"z": lam // 4, "x": pl.ds(lax.rem(lam, 2) * 2, 2), "y": slice(None)}
        v = dparts[p][pos[o[2]], lax.rem(lam // 2, 2), pos[o[1]], pos[o[0]], :, cols]
        if o.index("y") > o.index("x"):
            v = jnp.swapaxes(v, 0, 1)
        return v.reshape(128, v.shape[-1])

    def step1():
        for p in ps:
            while sib_wait[p]:
                d_wait(*sib_wait[p].pop(0))

        @pl.loop(0, 8 // pg)
        def _(g):
            for q in range(pg):
                t_gather(g * pg + q)
            if not opt["S1"]:
                return

            for t in range(2):
                lams = [lam_ref[t, k] for k in range(4)]
                lhs = tl[t, pl.ds(pl.multiple_of(g * pg * 128, pg * 128), pg * 128)]
                for p in ps:
                    _, first, width = parts[p]
                    for start in range(0, width, 512):
                        nc = min(512, width - start)
                        rhs = jnp.concatenate([lam_rows(p, lam, pl.ds(start, nc)) for lam in lams], axis=0)
                        res = jnp.dot(lhs, rhs, preferred_element_type=F32).astype(BF16)
                        for q in range(pg):
                            for h in range(nc // 128):
                                prod[g * pg + q, (first + start) // 128 + h, :, pl.ds(t * 128, 128)] = (
                                    res[q * 128:(q + 1) * 128, h * 128:(h + 1) * 128].T)

    acts = {"1": stage1, "1b": stage1b, "2": stage2, "3": stage3, "4": stage4, "T": t_start, "S": step1, "C": c_start}
    used = set(opt["sched"])
    for name, *arg in opt["sched"]:
        acts[name](*arg)
    for p in ps:
        if ("1b", p) not in used:
            own_d[p].wait()
    if ("C",) in used:
        for p in range(8):
            pltpu.make_async_copy(c_hbm.at[p], cbuf.at[p], c_sem.at[p]).wait()

    def step2(nu):
        if not opt["S2"]:
            return jnp.zeros((128, 256), F32)
        sigs = [sig_ref[k, nu] for k in range(4)]
        lhs = jnp.concatenate([cbuf[p, nu, k] for p in range(8) for k in range(4)], axis=1)
        rhs = jnp.concatenate([prod[p, s] for p in range(8) for s in sigs], axis=0)
        return jnp.dot(lhs, rhs, preferred_element_type=F32)

    def spot(dx, dy):
        return lax.rem(x + dx + 4, 4) * 4 + lax.rem(y + dy + 4, 4)

    def mid_copy(s, nu, slot, dst):
        return pltpu.make_async_remote_copy(src_ref=kbf.at[nu], dst_ref=kmid.at[slot], send_sem=k_send.at[s], recv_sem=m_recv.at[slot],
                                            device_id=(r, dst), device_id_type=MESH)

    def own_copy(src_ref, s, dst, src):
        return pltpu.make_async_remote_copy(src_ref=src_ref, dst_ref=krecv.at[src], send_sem=k_send.at[s], recv_sem=k_recv.at[src],
                                            device_id=(r, dst), device_id_type=MESH)

    FIRST = 7

    def send(i, dx, dy, nu):
        @pl.when((i < 4) & (dx != 0))
        def _():
            mid_copy(i, nu, dx - 1, spot(dx, 0)).start()

        @pl.when((i >= 4) & (i < FIRST) & (dy != 0))
        def _():
            mid_copy(i, nu, 3 + dy // 2, spot(0, dy)).start()

        @pl.when((i >= FIRST) & (i < 15))
        def _():
            own_copy(kbf.at[nu], i, nu, c).start()

        @pl.when(i == opt["mid"])
        def _():
            for slot in range(5):
                pltpu.make_async_copy(kmid.at[slot], kmid.at[slot], m_recv.at[slot]).wait()
            for j, (slots, at) in enumerate((((0, 1, 2), spot(0, 2)), ((3, 4), spot(2, 0)))):
                tot = kbf[at].astype(F32)
                for slot in slots:
                    tot += kmid[slot].astype(F32)
                ksum[j] = tot.astype(BF16)
                own_copy(ksum.at[j], 16 + j, at, c).start()

    def two_nus(i, carry):
        cx, cy = carry
        at = [(cx % 4, cy % 4), (cx // 4 % 4, cy // 4 % 4)]
        nus = [spot(*v) for v in at]
        accs = [step2(nu) for nu in nus]
        for nu, acc in zip(nus, accs):
            kbf[nu] = acc.astype(BF16)
        if opt["K"]:
            for j in range(2):
                send(2 * i + j, *at[j], nus[j])

        @pl.when(i == 7)
        def _():
            out_ref[...] = accs[1]

        return cx // 16, cy // 16

    SEQ = ((1, 2), (2, 2), (3, 2), (0, 2), (2, 1), (2, 3), (2, 0), (1, 1), (3, 3), (1, 3), (3, 1), (1, 0), (0, 1), (3, 0), (0, 3))
    lax.fori_loop(0, 8, two_nus, tuple(jnp.int32(sum(v[a] * 4**i for i, v in enumerate(SEQ))) for a in range(2)))

    for cp in started:
        cp.wait_send()
    for p in range(8):
        if any(u[0] == "T" for u in used):
            pltpu.make_async_copy(rbuf.at[pl.ds(0, 15), p], rbuf.at[pl.ds(0, 15), p], t_send.at[p]).wait()

    if opt["K"]:
        last = SEQ[FIRST:] + ((0, 2), (2, 0))
        for dx, dy in last:
            src = spot(-dx, -dy)
            own_copy(ksum.at[0], 0, c, src).wait_recv()
            out_ref[...] += krecv[src].astype(F32)
        for i, (dx, dy) in enumerate(SEQ):
            if (dx, dy) not in ((0, 2), (2, 0)):
                pltpu.make_async_copy(kbf.at[0], kbf.at[0], k_send.at[i]).wait()
        for j in range(2):
            pltpu.make_async_copy(kbf.at[0], kbf.at[0], k_send.at[16 + j]).wait()


def per_device(opt, tensor_blocks, density, coef, lam_list, sig_list):
    parts = opt["parts"]
    return pl.pallas_call(
        functools.partial(kernel, opt),
        out_shape=jax.ShapeDtypeStruct((128, 256), F32),
        in_specs=[pl.BlockSpec(memory_space=pltpu.SMEM)] * 2 + [pl.BlockSpec(memory_space=pl.ANY)] * 3,
        out_specs=pl.BlockSpec(memory_space=pltpu.VMEM),
        scratch_shapes=[
            pltpu.VMEM((8, 16, 4, 128, 128), BF16),
            pltpu.VMEM((16, 8, 64, 128), BF16),
            pltpu.VMEM((2, 1024, 512), BF16),
            pltpu.VMEM((8, 16, 128, 256), BF16),
            pltpu.VMEM((16, 128, 256), BF16),
            pltpu.VMEM((16, 128, 256), BF16),
            pltpu.SemaphoreType.DMA((16 * len(parts),)),
            pltpu.SemaphoreType.DMA((16 * len(parts),)),
            pltpu.SemaphoreType.DMA((8,)),
            pltpu.SemaphoreType.DMA((8,)),
            pltpu.SemaphoreType.DMA((18,)),
            pltpu.SemaphoreType.DMA((16,)),
            pltpu.SemaphoreType.DMA((len(parts),)),
            pltpu.SemaphoreType.DMA((8,)),
            pltpu.VMEM((5, 128, 256), BF16),
            pltpu.VMEM((2, 128, 256), BF16),
            pltpu.SemaphoreType.DMA((5,)),
        ] + [pltpu.VMEM((4, 2, 4, 4, 16, width), BF16) for _, _, width in parts],
        compiler_params=pltpu.CompilerParams(collective_id=0, has_side_effects=True, vmem_limit_bytes=60 * 2**20),
        cost_estimate=pl.CostEstimate(flops=2**33, bytes_accessed=20 * 2**20, transcendentals=0),
    )(lam_list, sig_list.T, tensor_blocks.reshape(128, 64, 128), density, coef)


def solution(mesh, **kw):
    in_specs = (
        P(None, "row", None, "col", None),
        P(("row", "col"), None),
        P("col", None, None, None, None),
        P("row", None),
        P(),
    )
    return jax.shard_map(functools.partial(per_device, {**OPT, **kw}), mesh=mesh, in_specs=in_specs, out_specs=P("col", "row"), check_vma=False)
```

time: 255 us -> 67.1 us (0.26)
  waiting for transfers between devices: 147 us -> 0 us
  Pallas kernels: 0 us -> 65.4 us
  local copies, waits for them, and re-layouts: 52.4 us -> 1.57 us
  matrix products: 30.7 us -> 0 us
  between operations: 13.4 us -> 0.01 us
  starting transfers between devices: 7.64 us -> 0 us
    all_gather x1 -> x0, waiting for transfers between devices: 76.7 us -> none  [per_device(): gathered = lax.all_gather(density, ('row', 'col'), axis=0, tiled=True)]
    reduce_scatter x1 -> x0, waiting for transfers between devices: 69.8 us -> none  [per_device(): lax.psum_scatter(partial_sum.reshape(basis_count, mu_rows), 'col', scatte...]
    pallas_call x0 -> x1, Pallas kernels: none -> 65.4 us  [per_device(): pl.pallas_call(functools.partial(kernel, opt), out_shape=jax.ShapeDtypeSt...]
    dot_general x2 -> x0, matrix products: 30.7 us -> none  [the longest x1 20.3 us: per_device(): jnp.einsum('amukj,aukij->uim', picked, coef, preferred_element_type=jnp.f...]
    gather x2 -> x0, local copies, waits for them, and re-layouts: 21.9 us -> none  [the longest x1 15.8 us: per_device(): picked = jnp.take(by_tile, sig_list, axis=2)]
    convert_element_type x1 -> x0, local copies, waits for them, and re-layouts: 11.5 us -> none  [per_device(): jnp.einsum('atkij,tkjn->atin', blocks, tile_rows, preferred_element_type=...]
    reshape x1 -> x0, local copies, waits for them, and re-layouts: 8.93 us -> none  [per_device(): by_tile = products.reshape(aux_count, mu_rows, tile_count, tile_width)]
    unnamed x1, local copies, waits for them, and re-layouts: 9.77 us -> 1.57 us
  transfers between devices with their start and end apart: 3 -> 0, of which waited for: 2 -> 0; matrix products, arithmetic and copies ran while one was open for 3% -> 0% of each run, Pallas kernels for 0% -> 0%
where the time goes in v3:
time: 67.1 us; the launch traced here: 67 us
  Pallas kernels  65.4 us (97%)
  local copies, waits for them, and re-layouts  1.57 us (2%)
    pallas_call x1, Pallas kernels, per_device(): pl.pallas_call(functools.partial(kernel, opt), out_shape=jax.ShapeDtypeSt...  65.4 us
    unnamed x1, local copies, waits for them, and re-layouts  1.57 us

profile of v3, /device:TPU:1, one launch (start us, length us, event | category | flops | bytes accessed | tf_op | source)
XLA Modules:
  0.0 67.0 jit_solution(4645923749749665071)
XLA Ops:
  0.0 65.4 %shard_map.55 = f32[128,256]{1,0:T(8,128)} custom-call(s32[2,4]{1,0:T(2,128)} %lam_ref.1, s32[4,16]{1,0:T(4,128)} %bitcast.3, bf16[128,64,128]{2,1,0:T(8,128)(2,1)} %bitcast.2, bf16[16,2048]{1,0:T(8,128)(2,1)} %d_hbm.1, bf16[8,16,4,128,128]{4,3,2,1,0:T(8,128)(2,1)} %c_hbm.1), custom_call_target="tpu_custom_call" | custom-call | flops 8589934592 | bytes 20971520 | tf_op jit(solution)/shard_map/pallas_call | solution.py:284
  65.4 1.6 %copy.7 = f32[128,256]{1,0:T(8,128)} copy(f32[128,256]{1,0:T(8,128)} %shard_map.55) | data formatting | bytes 262144

commit v4 on v3

--- a/solution.py
+++ b/solution.py
@@ -283,7 +283,7 @@
     parts = opt["parts"]
     return pl.pallas_call(
         functools.partial(kernel, opt),
-        out_shape=jax.ShapeDtypeStruct((128, 256), F32),
+        out_shape=pltpu.VMEM((128, 256), F32),
         in_specs=[pl.BlockSpec(memory_space=pltpu.SMEM)] * 2 + [pl.BlockSpec(memory_space=pl.ANY)] * 3,
         out_specs=pl.BlockSpec(memory_space=pltpu.VMEM),
         scratch_shapes=[

time: 67.1 us -> 65.6 us (0.978)
  local copies, waits for them, and re-layouts: 1.57 us -> 0.66 us
    unnamed x1, local copies, waits for them, and re-layouts: 1.57 us -> 0.66 us
where the time goes in v4:
time: 65.6 us; the launch traced here: 65.4 us
  Pallas kernels  64.8 us (99%)
  local copies, waits for them, and re-layouts  0.66 us (1%)
    pallas_call x1, Pallas kernels, per_device(): pl.pallas_call(functools.partial(kernel, opt), out_shape=pltpu.VMEM((128,...  64.8 us

profile of v4, /device:TPU:1, one launch (start us, length us, event | category | flops | bytes accessed | tf_op | source)
XLA Modules:
  0.0 65.4 jit_solution(8319999500438389055)
XLA Ops:
  0.0 64.8 %shard_map.55 = f32[128,256]{1,0:T(8,128)S(1)} custom-call(s32[2,4]{1,0:T(2,128)} %lam_ref.1, s32[4,16]{1,0:T(4,128)} %bitcast.3, bf16[128,64,128]{2,1,0:T(8,128)(2,1)} %bitcast.2, bf16[16,2048]{1,0:T(8,128)(2,1)} %d_hbm.1, bf16[8,16,4,128,128]{4,3,2,1,0:T(8,128)(2,1)} %c_hbm.1), custom_call_target="tpu_custom_call" | custom-call | flops 8589934592 | bytes 20971520 | tf_op jit(solution)/shard_map/pallas_call | solution.py:284
  64.8 0.7 %copy.7 = f32[128,256]{1,0:T(8,128)} copy(f32[128,256]{1,0:T(8,128)S(1)} %shard_map.55) | data formatting | bytes 262144

commit v5 on v4

--- a/solution.py
+++ b/solution.py
@@ -12,7 +12,7 @@
 PARTS = (("xyz", 0, 768), ("yxz", 768, 768), ("zxy", 1536, 256), ("zyx", 1792, 256))
 ORDER = tuple(((i + i // 4) % 4, i % 4) for i in range(1, 16))
 SCHED = (("1", 0), ("1", 1), ("1", 2), ("1", 3), ("1b", 0), ("1b", 1), ("1b", 2), ("1b", 3), ("T", 0, 2), ("2", 0), ("2", 1), ("2", 2), ("2", 3),
-         ("T", 2, 4), ("C",), ("3", 2), ("3", 3), ("T", 4, 8), ("3", 0), ("3", 1), ("4", 2), ("4", 3), ("4", 0), ("4", 1), ("S",))
+         ("T", 2, 4), ("C",), ("3", 2), ("3", 3), ("T", 4, 8), ("3", 0), ("3", 1), ("4", 2), ("4", 3), ("G",), ("4", 0), ("4", 1), ("S",))
 OPT = dict(S1=True, S2=True, K=True, pg=4, parts=PARTS, sched=SCHED, order=ORDER, bar=False, mid=13)
 
 
@@ -165,8 +165,11 @@
 
         @pl.loop(0, 8 // pg)
         def _(g):
-            for q in range(pg):
-                t_gather(g * pg + q)
+            @pl.when(g > 0)
+            def _():
+                for q in range(pg):
+                    t_gather(g * pg + q)
+
             if not opt["S1"]:
                 return
 
@@ -184,7 +187,10 @@
                                 prod[g * pg + q, (first + start) // 128 + h, :, pl.ds(t * 128, 128)] = (
                                     res[q * 128:(q + 1) * 128, h * 128:(h + 1) * 128].T)
 
-    acts = {"1": stage1, "1b": stage1b, "2": stage2, "3": stage3, "4": stage4, "T": t_start, "S": step1, "C": c_start}
+    def gather_first():
+        pl.loop(0, pg)(t_gather)
+
+    acts = {"G": gather_first, "1": stage1, "1b": stage1b, "2": stage2, "3": stage3, "4": stage4, "T": t_start, "S": step1, "C": c_start}
     used = set(opt["sched"])
     for name, *arg in opt["sched"]:
         acts[name](*arg)

time: 65.6 us -> 65.6 us (level)
  no operation moved by 1% of the time
where the time goes in v5:
time: 65.6 us; the launch traced here: 65.4 us
  Pallas kernels  64.8 us (99%)
  local copies, waits for them, and re-layouts  0.66 us (1%)
    pallas_call x1, Pallas kernels, per_device(): pl.pallas_call(functools.partial(kernel, opt), out_shape=pltpu.VMEM((128,...  64.8 us

profile of v5, /device:TPU:1, one launch (start us, length us, event | category | flops | bytes accessed | tf_op | source)
XLA Modules:
  0.0 65.4 jit_solution(17033893911915002465)
XLA Ops:
  0.0 64.8 %shard_map.55 = f32[128,256]{1,0:T(8,128)S(1)} custom-call(s32[2,4]{1,0:T(2,128)} %lam_ref.1, s32[4,16]{1,0:T(4,128)} %bitcast.3, bf16[128,64,128]{2,1,0:T(8,128)(2,1)} %bitcast.2, bf16[16,2048]{1,0:T(8,128)(2,1)} %d_hbm.1, bf16[8,16,4,128,128]{4,3,2,1,0:T(8,128)(2,1)} %c_hbm.1), custom_call_target="tpu_custom_call" | custom-call | flops 8589934592 | bytes 20971520 | tf_op jit(solution)/shard_map/pallas_call | solution.py:290
  64.8 0.7 %copy.7 = f32[128,256]{1,0:T(8,128)} copy(f32[128,256]{1,0:T(8,128)S(1)} %shard_map.55) | data formatting | bytes 262144
